TPU v7x, 256 devices: a whole 4x4x8 slice. The times are simulated.
256 devices in a mesh: gx: 4 (over y), yz: 64 (over z, x, core).
Axes of the slice: x: 4, y: 4, z: 8, core: 2. Of those that a mesh axis runs over, the one named last changes fastest.
Arguments:
- potential: float32 [32, 512, 2048], P('gx', 'yz'), may hold values from -96 to 96
- gal_cells: int32 [4, 64, 64, 128], P('gx', 'yz'), may hold values from 0 to 63
- gal_z: int32 [4, 64, 64, 128], P('gx', 'yz'), may hold values from 0 to 2047
- gal_bins: int32 [4, 64, 64, 128], P('gx', 'yz'), may hold values from 0 to 7
- gal_counts: int32 [4, 64, 64], P('gx', 'yz'), may hold values from 1 to 128, as said below
Outputs:
- tidal: float32 [6, 4, 64, 8192], P(None, 'gx', 'yz')
Inputs may be any that keep to these rules, and one draw needn't show every extreme that they name: For each band g, one tile d receives 128 live slots from every home device; the live slots are the first gal_counts ones.
All inputs are finite; a program needn't handle non-finite values.
Results may differ from a plain program's by a relative error of at most 0.00002.
Values sent between devices are 32-bit elements; how exact they have to be, the bound alone decides.
A program may use at most 192 MiB of HBM per device.

v0:
```python
import jax
import jax.numpy as jnp
from jax import lax
from jax.sharding import PartitionSpec as P

HALO = 6
BINS = 8


def padded_2(shard, sides, width):
    for axis, dim in sides:
        size, length = (lax.axis_size(axis), shard.shape[dim])
        up = [(i, (i + 1) % size) for i in range(size - 1)]
        down = [(j, i) for i, j in up]
        last = lax.slice_in_dim(shard, length - width, length, axis=dim)
        initial = lax.slice_in_dim(shard, 0, width, axis=dim)
        before = lax.ppermute(last, axis, up)
        after = lax.ppermute(initial, axis, down)
        shard = jnp.concatenate([before, shard, after], axis=dim)
    return shard


def kernels():
    offsets = jnp.arange(-HALO, HALO + 1).astype(jnp.float32)
    sigma_cells = HALO / 3.0
    smooth_w = jnp.exp(-offsets * offsets / (2.0 * sigma_cells * sigma_cells))
    smooth_w = smooth_w / jnp.sum(smooth_w)
    first_w = offsets / (sigma_cells * sigma_cells) * smooth_w
    second_w = (offsets * offsets / sigma_cells**4 - 1.0 / (sigma_cells * sigma_cells)) * smooth_w
    return (smooth_w, first_w, second_w)


def sweep_axis(padded, weights, axis):
    length = padded.shape[axis] - 2 * HALO
    summed = weights[0] * lax.slice_in_dim(padded, 0, length, axis=axis)
    for k in range(1, 2 * HALO + 1):
        summed = summed + weights[k] * lax.slice_in_dim(padded, k, k + length, axis=axis)
    return summed


def tensor_fields(along_x, weights):
    x_smooth, x_first, x_second = along_x
    smooth_w, first_w, second_w = weights
    plans = [
        (x_second, smooth_w, smooth_w),
        (x_smooth, second_w, smooth_w),
        (x_smooth, smooth_w, second_w),
        (x_first, first_w, smooth_w),
        (x_first, smooth_w, first_w),
        (x_smooth, first_w, first_w),
    ]
    results = []
    for field, y_w, z_w in plans:
        in_y = sweep_axis(field, y_w, 1)
        wrapped = jnp.concatenate([in_y[:, :, -HALO:], in_y, in_y[:, :, :HALO]], axis=2)
        results.append(sweep_axis(wrapped, z_w, 2))
    return jnp.stack(results)


def look_up(flat_tensor, z_depth, slot_cells, slot_zeds, slot_bins):
    scale = (HALO / 3.0) ** 2
    here_cell = slot_cells * z_depth + slot_zeds
    next_cell = slot_cells * z_depth + (slot_zeds + 1) % z_depth
    here_value = jnp.take(flat_tensor, here_cell.reshape(-1), axis=1).reshape(
        (6,) + slot_cells.shape
    )
    next_value = jnp.take(flat_tensor, next_cell.reshape(-1), axis=1).reshape(
        (6,) + slot_cells.shape
    )
    weight = (slot_bins.astype(jnp.float32) + 0.5) / BINS
    return ((1.0 - weight) * here_value + weight * next_value) * scale


def build_tensor(potential, weights):
    padded = padded_2(potential, (("gx", 0), ("yz", 1)), HALO)
    along_x = [sweep_axis(padded, w, 0) for w in weights]
    components = tensor_fields(along_x, weights)
    return components.reshape(6, -1)


def body(potential, gal_cells, gal_z, gal_bins, gal_counts):
    weights = kernels()
    z_depth = potential.shape[2]
    tiles = gal_cells.shape[2]
    slots = gal_cells.shape[3]
    slot_cells = gal_cells.reshape(tiles, slots)
    slot_zeds = gal_z.reshape(tiles, slots)
    slot_bins = gal_bins.reshape(tiles, slots)
    flat_tensor = build_tensor(potential, weights)
    served = look_up(
        flat_tensor,
        z_depth,
        lax.all_to_all(slot_cells, "yz", split_axis=0, concat_axis=0, tiled=True),
        lax.all_to_all(slot_zeds, "yz", split_axis=0, concat_axis=0, tiled=True),
        lax.all_to_all(slot_bins, "yz", split_axis=0, concat_axis=0, tiled=True),
    )
    returned = lax.all_to_all(served, "yz", split_axis=1, concat_axis=1, tiled=True)
    slot_index = lax.broadcasted_iota(jnp.int32, (tiles, slots), 1)
    live = slot_index < gal_counts.reshape(tiles, 1)
    tidal = jnp.where(live[None], returned, jnp.float32(0.0))
    return tidal.reshape(6, 1, 1, tiles * slots)


def solution(mesh):
    return jax.shard_map(
        body,
        mesh=mesh,
        in_specs=(
            P("gx", "yz", None),
            P("gx", "yz", None, None),
            P("gx", "yz", None, None),
            P("gx", "yz", None, None),
            P("gx", "yz", None),
        ),
        out_specs=P(None, "gx", "yz", None),
        check_vma=False,
    )
```

profile of v0, /device:TPU:1, one launch (start us, length us, event | category | flops | bytes accessed | tf_op | source)
XLA Modules:
  0.0 547.2 jit_solution(1780503978091205274)
XLA Ops:
  0.0 1.3 copy.27
  1.4 4.1 collective-permute-start
  5.5 1.3 collective-permute-start.1
  6.8 12.4 %all-to-all-start = ((s32[64,1,128]{2,1,0:T(1,128)}), s32[64,1,128]{2,1,0:T(1,128)S(1)}, u32[]{:S(2)}, u32[]{:S(2)}) async-start(s32[64,1,128]{2,1,0:T(1,128)} %bitcast.1), calls=%async_computation | async-start | bytes 65536 | tf_op jit(solution)/shard_map/all_to_all | solution.py:95
  23.6 1.7 fusion.221
  25.3 3.5 collective-permute-start.2
  28.8 1.9 collective-permute-start.3
  30.7 11.3 %all-to-all-start.1 = ((s32[64,1,128]{2,1,0:T(1,128)}), s32[64,1,128]{2,1,0:T(1,128)S(1)}, u32[]{:S(2)}, u32[]{:S(2)}) async-start(s32[64,1,128]{2,1,0:T(1,128)} %bitcast.3), calls=%async_computation.1 | async-start | bytes 65536 | tf_op jit(solution)/shard_map/all_to_all | solution.py:93
  42.1 9.2 %all-to-all-done.1 = s32[64,1,128]{2,1,0:T(1,128)S(1)} async-done(((s32[64,1,128]{2,1,0:T(1,128)}), s32[64,1,128]{2,1,0:T(1,128)S(1)}, u32[]{:S(2)}, u32[]{:S(2)}) %all-to-all-start.1) | async-done | bytes 32800 | tf_op jit(solution)/shard_map/all_to_all | solution.py:93
  51.3 8.7 %all-to-all-start.2 = ((s32[64,1,128]{2,1,0:T(1,128)}), s32[64,1,128]{2,1,0:T(1,128)S(1)}, u32[]{:S(2)}, u32[]{:S(2)}) async-start(s32[64,1,128]{2,1,0:T(1,128)} %bitcast.5), calls=%async_computation.2 | async-start | bytes 65536 | tf_op jit(solution)/shard_map/all_to_all | solution.py:94
  60.1 9.3 %all-to-all-done.2 = s32[64,1,128]{2,1,0:T(1,128)S(1)} async-done(((s32[64,1,128]{2,1,0:T(1,128)}), s32[64,1,128]{2,1,0:T(1,128)S(1)}, u32[]{:S(2)}, u32[]{:S(2)}) %all-to-all-start.2) | async-done | bytes 32800 | tf_op jit(solution)/shard_map/all_to_all | solution.py:94
  69.5 1.7 pad_maximum_fusion
  71.2 10.2 %multiply_add_fusion.1 = f32[8,20,2048]{2,0,1:T(8,128)S(1)} fusion(f32[20,20,2048]{2,0,1:T(8,128)S(1)} %pad_maximum_fusion, f32[]{:T(128)} %bitcast.32, f32[]{:T(128)} %bitcast.31, f32[]{:T(128)} %bitcast.30, f32[]{:T(128)} %bitcast.29, f32[]{:T(128)} %bitcast.28, f32[]{:T(128)} %bitcast.27, f32[]{:T(128)} %bitcast.26, f32[]{:T(128)} %bitcast.25, ...), kind=kLoop, calls=%fused_computation.67 | loop fusion | flops 8192000 | bytes 18350132 | tf_op jit(solution)/shard_map/add | solution.py:37
  81.4 10.3 %multiply_add_fusion = f32[8,20,2048]{2,0,1:T(8,128)S(1)} fusion(f32[20,20,2048]{2,0,1:T(8,128)S(1)} %pad_maximum_fusion, f32[]{:T(128)} %bitcast.45, f32[]{:T(128)} %bitcast.44, f32[]{:T(128)} %bitcast.43, f32[]{:T(128)} %bitcast.42, f32[]{:T(128)} %bitcast.41, f32[]{:T(128)} %bitcast.40, f32[]{:T(128)} %bitcast.39, f32[]{:T(128)} %bitcast.38, f32[]{:T(128)} %bitcast.37, ...), kind=kLoop, calls=%fused_computation.66 | loop fusion | flops 8192000 | bytes 18350132 | tf_op jit(solution)/shard_map/add | solution.py:37
  91.8 8.6 %multiply_add_fusion.4 = f32[8,8,2048]{2,0,1:T(8,128)S(1)} fusion(f32[8,20,2048]{2,0,1:T(8,128)S(1)} %multiply_add_fusion, f32[]{:T(128)} %bitcast.32, f32[]{:T(128)} %bitcast.31, f32[]{:T(128)} %bitcast.30, f32[]{:T(128)} %bitcast.29, f32[]{:T(128)} %bitcast.28, f32[]{:T(128)} %bitcast.27, f32[]{:T(128)} %bitcast.26, f32[]{:T(128)} %bitcast.25, ...), kind=kLoop, calls=%fused_computation.347 | loop fusion | flops 3276800 | bytes 7340084 | tf_op jit(solution)/shard_map/add | solution.py:37
  100.3 8.7 %multiply_add_fusion.5 = f32[8,8,2048]{2,0,1:T(8,128)S(1)} fusion(f32[8,20,2048]{2,0,1:T(8,128)S(1)} %multiply_add_fusion, f32[]{:T(128)} %bitcast.45, f32[]{:T(128)} %bitcast.44, f32[]{:T(128)} %bitcast.43, f32[]{:T(128)} %bitcast.42, f32[]{:T(128)} %bitcast.41, f32[]{:T(128)} %bitcast.40, f32[]{:T(128)} %bitcast.39, f32[]{:T(128)} %bitcast.38, ...), kind=kLoop, calls=%fused_computation.348 | loop fusion | flops 3276800 | bytes 7340084 | tf_op jit(solution)/shard_map/add | solution.py:37
  109.1 8.7 %multiply_add_fusion.3 = f32[8,8,2048]{2,0,1:T(8,128)S(1)} fusion(f32[8,20,2048]{2,0,1:T(8,128)S(1)} %multiply_add_fusion.1, f32[]{:T(128)} %bitcast.45, f32[]{:T(128)} %bitcast.44, f32[]{:T(128)} %bitcast.43, f32[]{:T(128)} %bitcast.42, f32[]{:T(128)} %bitcast.41, f32[]{:T(128)} %bitcast.40, f32[]{:T(128)} %bitcast.39, f32[]{:T(128)} %bitcast.38, ...), kind=kLoop, calls=%fused_computation.346 | loop fusion | flops 3276800 | bytes 7340084 | tf_op jit(solution)/shard_map/add | solution.py:37
  117.8 8.6 %multiply_add_fusion.6 = f32[8,8,2048]{2,0,1:T(8,128)S(1)} fusion(f32[8,20,2048]{2,0,1:T(8,128)S(1)} %multiply_add_fusion.1, f32[]{:T(128)} %bitcast.32, f32[]{:T(128)} %bitcast.31, f32[]{:T(128)} %bitcast.30, f32[]{:T(128)} %bitcast.29, f32[]{:T(128)} %bitcast.28, f32[]{:T(128)} %bitcast.27, f32[]{:T(128)} %bitcast.26, f32[]{:T(128)} %bitcast.25, ...), kind=kLoop, calls=%fused_computation.349 | loop fusion | flops 3276800 | bytes 7340084 | tf_op jit(solution)/shard_map/add | solution.py:37
  126.4 8.3 %multiply_add_fusion.7 = f32[8,8,2048]{2,0,1:T(8,128)S(1)} fusion(f32[8,20,2048]{2,0,1:T(8,128)S(1)} %multiply_add_fusion.1, f32[]{:T(128)} %bitcast.20, f32[]{:T(128)} %bitcast.19, f32[]{:T(128)} %bitcast.18, f32[]{:T(128)} %bitcast.17, f32[]{:T(128)} %bitcast.16, f32[]{:T(128)} %bitcast.15, f32[]{:T(128)} %bitcast.14, f32[]{:T(128)} %bitcast.13, ...), kind=kLoop, calls=%fused_computation.350 | loop fusion | flops 3276800 | bytes 7340084 | tf_op jit(solution)/shard_map/add | solution.py:37
  134.7 10.1 %multiply_add_fusion.2 = f32[8,20,2048]{2,0,1:T(8,128)S(1)} fusion(f32[20,20,2048]{2,0,1:T(8,128)S(1)} %pad_maximum_fusion, f32[]{:T(128)} %bitcast.20, f32[]{:T(128)} %bitcast.19, f32[]{:T(128)} %bitcast.18, f32[]{:T(128)} %bitcast.17, f32[]{:T(128)} %bitcast.16, f32[]{:T(128)} %bitcast.15, f32[]{:T(128)} %bitcast.14, f32[]{:T(128)} %bitcast.13, ...), kind=kLoop, calls=%fused_computation.68 | loop fusion | flops 8192000 | bytes 18350132 | tf_op jit(solution)/shard_map/add | solution.py:37
  144.9 10.1 %fusion.3 = f32[8,8,2048]{2,0,1:T(8,128)S(1)} fusion(f32[8,8,6]{2,0,1:T(8,128)S(1)} %get-tuple-element.9, f32[8,8,6]{2,0,1:T(8,128)S(1)} %get-tuple-element.8, f32[8,8,2048]{2,0,1:T(8,128)S(1)} %multiply_add_fusion.3, f32[]{:T(128)} %bitcast.45, f32[]{:T(128)} %bitcast.44, f32[]{:T(128)} %bitcast.43, f32[]{:T(128)} %bitcast.42, f32[]{:T(128)} %bitcast.41, ...), kind=kLoop, calls=%fused_computation.72 | loop fusion | flops 4849664 | bytes 1051700 | tf_op jit(solution)/shard_map/add | solution.py:37
  155.0 1.1 copy.35
  156.1 2.5 stack.26
  158.7 10.1 %fusion.35 = f32[8,8,2048]{2,0,1:T(8,128)S(1)} fusion(f32[8,8,6]{2,0,1:T(8,128)S(1)} %get-tuple-element.11, f32[8,8,6]{2,0,1:T(8,128)S(1)} %get-tuple-element.10, f32[8,8,2048]{2,0,1:T(8,128)S(1)} %multiply_add_fusion.4, f32[]{:T(128)} %bitcast.45, f32[]{:T(128)} %bitcast.44, f32[]{:T(128)} %bitcast.43, f32[]{:T(128)} %bitcast.42, f32[]{:T(128)} %bitcast.41, ...), kind=kLoop, calls=%fused_computation.104 | loop fusion | flops 4849664 | bytes 1051700 | tf_op jit(solution)/shard_map/add | solution.py:37
  168.8 1.1 copy.34
  169.9 1.7 stack.25
  171.6 9.9 %fusion.67 = f32[8,8,2048]{2,0,1:T(8,128)S(1)} fusion(f32[8,8,6]{2,0,1:T(8,128)S(1)} %get-tuple-element.13, f32[8,8,6]{2,0,1:T(8,128)S(1)} %get-tuple-element.12, f32[8,8,2048]{2,0,1:T(8,128)S(1)} %multiply_add_fusion.5, f32[]{:T(128)} %bitcast.32, f32[]{:T(128)} %bitcast.31, f32[]{:T(128)} %bitcast.30, f32[]{:T(128)} %bitcast.29, f32[]{:T(128)} %bitcast.28, ...), kind=kLoop, calls=%fused_computation.136 | loop fusion | flops 4849664 | bytes 1051700 | tf_op jit(solution)/shard_map/add | solution.py:37
  181.5 1.1 copy.33
  182.6 1.7 stack.24
  184.4 9.7 %fusion.99 = f32[8,8,2048]{2,0,1:T(8,128)S(1)} fusion(f32[8,8,6]{2,0,1:T(8,128)S(1)} %get-tuple-element.15, f32[8,8,6]{2,0,1:T(8,128)S(1)} %get-tuple-element.14, f32[8,8,2048]{2,0,1:T(8,128)S(1)} %multiply_add_fusion.6, f32[]{:T(128)} %bitcast.20, f32[]{:T(128)} %bitcast.19, f32[]{:T(128)} %bitcast.18, f32[]{:T(128)} %bitcast.17, f32[]{:T(128)} %bitcast.16, ...), kind=kLoop, calls=%fused_computation.168 | loop fusion | flops 4849664 | bytes 1051700 | tf_op jit(solution)/shard_map/add | solution.py:37
  194.1 1.1 copy.32
  195.2 1.7 stack.23
  196.9 10.1 %fusion.131 = f32[8,8,2048]{2,0,1:T(8,128)S(1)} fusion(f32[8,8,6]{2,0,1:T(8,128)S(1)} %get-tuple-element.17, f32[8,8,6]{2,0,1:T(8,128)S(1)} %get-tuple-element.16, f32[8,8,2048]{2,0,1:T(8,128)S(1)} %multiply_add_fusion.7, f32[]{:T(128)} %bitcast.32, f32[]{:T(128)} %bitcast.31, f32[]{:T(128)} %bitcast.30, f32[]{:T(128)} %bitcast.29, f32[]{:T(128)} %bitcast.28, ...), kind=kLoop, calls=%fused_computation.200 | loop fusion | flops 4849664 | bytes 1051700 | tf_op jit(solution)/shard_map/add | solution.py:37
  208.2 1.7 stack.22
  209.8 8.6 %fusion.204 = f32[8,8,2048]{2,0,1:T(8,128)S(1)} fusion(f32[8,20,2048]{2,0,1:T(8,128)S(1)} %multiply_add_fusion.2, f32[]{:T(128)} %bitcast.32, f32[]{:T(128)} %bitcast.31, f32[]{:T(128)} %bitcast.30, f32[]{:T(128)} %bitcast.29, f32[]{:T(128)} %bitcast.28, f32[]{:T(128)} %bitcast.27, f32[]{:T(128)} %bitcast.26, f32[]{:T(128)} %bitcast.25, f32[]{:T(128)} %bitcast.24, ...), kind=kLoop, calls=%fused_computation.322 | loop fusion | flops 3276800 | bytes 7340084 | tf_op jit(solution)/shard_map/add | solution.py:37
  218.5 9.9 %fusion.163 = f32[8,8,2048]{2,0,1:T(8,128)S(1)} fusion(f32[8,8,6]{2,0,1:T(8,128)S(1)} %get-tuple-element.19, f32[8,8,6]{2,0,1:T(8,128)S(1)} %get-tuple-element.18, f32[8,8,2048]{2,0,1:T(8,128)S(1)} %fusion.204, f32[]{:T(128)} %bitcast.32, f32[]{:T(128)} %bitcast.31, f32[]{:T(128)} %bitcast.30, f32[]{:T(128)} %bitcast.29, f32[]{:T(128)} %bitcast.28, ...), kind=kLoop, calls=%fused_computation.232 | loop fusion | flops 4849664 | bytes 1051700 | tf_op jit(solution)/shard_map/add | solution.py:37
  228.4 1.1 copy.30
  229.5 1.7 stack.21
  231.2 8.1 %stack.27 = f32[6,131072]{1,0:T(8,128)} concatenate(f32[1,131072]{1,0:T(1,128)S(1)} %stack.21, f32[1,131072]{1,0:T(1,128)S(1)} %stack.22, f32[1,131072]{1,0:T(1,128)S(1)} %stack.23, f32[1,131072]{1,0:T(1,128)S(1)} %stack.24, f32[1,131072]{1,0:T(1,128)S(1)} %stack.25, f32[1,131072]{1,0:T(1,128)S(1)} %copy-done), dimensions={0} | concatenate | bytes 6291456 | tf_op jit(solution)/shard_map/stack | solution.py:57
  239.3 30.2 %copy.36 = f32[6,131072]{0,1:T(8,128)} copy(f32[6,131072]{1,0:T(8,128)} %stack.27) | data formatting | bytes 6291456 | tf_op jit(solution)/shard_map/stack | solution.py:57
  269.6 118.5 %gather_fusion = f32[8192,6]{1,0:T(8,128)} fusion(f32[6,131072]{0,1:T(8,128)} %copy.36, s32[8192]{0:T(1024)S(1)} %get-tuple-element.24), kind=kCustom, calls=%fused_computation.clone | custom fusion | bytes 425984 | tf_op jit(solution)/shard_map/jit(_take)/gather | solution.py:64
  388.1 7.5 %broadcast_select_fusion.1 = f32[8192,6]{1,0:T(8,128)} fusion(f32[8192,6]{1,0:T(8,128)} %gather_fusion, pred[8192]{0:T(1024)(128)(4,1)S(1)} %get-tuple-element.22), kind=kLoop, calls=%fused_computation.4 | loop fusion | flops 49152 | bytes 401408 | tf_op jit(solution)/shard_map/jit(_take)/select_n | solution.py:64
  395.5 2.8 copy.37
  398.4 118.7 %gather_fusion.1 = f32[8192,6]{1,0:T(8,128)} fusion(f32[6,131072]{0,1:T(8,128)} %copy.36, s32[8192]{0:T(1024)S(1)} %get-tuple-element.25), kind=kCustom, calls=%fused_computation.1.clone | custom fusion | bytes 425984 | tf_op jit(solution)/shard_map/jit(_take)/gather | solution.py:67
  517.1 7.5 %broadcast_select_fusion = f32[8192,6]{1,0:T(8,128)} fusion(f32[8192,6]{1,0:T(8,128)} %gather_fusion.1, pred[8192]{0:T(1024)(128)(4,1)S(1)} %get-tuple-element.23), kind=kLoop, calls=%fused_computation.3 | loop fusion | flops 49152 | bytes 401408 | tf_op jit(solution)/shard_map/jit(_take)/select_n | solution.py:67
  524.5 2.8 copy.39
  528.1 4.8 all-to-all-start.3
  533.1 13.2 %all-to-all-done.3 = f32[6,64,128]{2,0,1:T(8,128)S(1)} async-done(((f32[6,64,128]{2,0,1:T(8,128)}), f32[6,64,128]{2,0,1:T(8,128)S(1)}, u32[]{:S(2)}, u32[]{:S(2)}) %all-to-all-start.3) | async-done | bytes 196640 | tf_op jit(solution)/shard_map/all_to_all | solution.py:97
  (33 shorter events, 7.9 us)
Async XLA Ops:
  1.4 21.9 %collective-permute-start = (f32[6,8,2048]{2,0,1:T(8,128)S(1)}, f32[6,8,2048]{2,0,1:T(8,128)S(1)}, u32[]{:S(2)}, u32[]{:S(2)}) collective-permute-start(f32[6,8,2048]{2,0,1:T(8,128)S(1)} %get-tuple-element.20), channel_id=1, source_target_pairs={{0,64},{64,128},{128,192},{1,65},{65,129},{129,193},{2,66},{66,130... | collective-permute-start | bytes 1179656 | tf_op jit(solution)/shard_map/ppermute | solution.py:17
  5.5 17.8 %collective-permute-start.1 = (f32[6,8,2048]{2,0,1:T(8,128)S(1)}, f32[6,8,2048]{2,0,1:T(8,128)S(1)}, u32[]{:S(2)}, u32[]{:S(2)}) collective-permute-start(f32[6,8,2048]{2,0,1:T(8,128)S(1)} %get-tuple-element.21), channel_id=1, source_target_pairs={{64,0},{128,64},{192,128},{65,1},{129,65},{193,129},{66,2},{130,66... | collective-permute-start | bytes 1179656 | tf_op jit(solution)/shard_map/ppermute | solution.py:18
  6.8 23.9 %all-to-all-start = ((s32[64,1,128]{2,1,0:T(1,128)}), s32[64,1,128]{2,1,0:T(1,128)S(1)}, u32[]{:S(2)}, u32[]{:S(2)}) async-start(s32[64,1,128]{2,1,0:T(1,128)} %bitcast.1), calls=%async_computation | async-start | bytes 65536 | tf_op jit(solution)/shard_map/all_to_all | solution.py:95
  25.3 44.2 %collective-permute-start.2 = (f32[20,6,2048]{2,0,1:T(8,128)}, f32[20,6,2048]{2,0,1:T(8,128)S(1)}, u32[]{:S(2)}, u32[]{:S(2)}) collective-permute-start(f32[20,6,2048]{2,0,1:T(8,128)} %get-tuple-element.6), channel_id=1, source_target_pairs={{0,1},{1,2},{2,3},{3,4},{4,5},{5,6},{6,7},{7,8},{8,9},{9,10},{10,1... | collective-permute-start | bytes 2949128 | tf_op jit(solution)/shard_map/ppermute | solution.py:17
  28.8 40.7 %collective-permute-start.3 = (f32[20,6,2048]{2,0,1:T(8,128)}, f32[20,6,2048]{2,0,1:T(8,128)}, u32[]{:S(2)}, u32[]{:S(2)}) collective-permute-start(f32[20,6,2048]{2,0,1:T(8,128)} %get-tuple-element.7), channel_id=1, source_target_pairs={{1,0},{2,1},{3,2},{4,3},{5,4},{6,5},{7,6},{8,7},{9,8},{10,9},{11,1... | collective-permute-start | bytes 2949128 | tf_op jit(solution)/shard_map/ppermute | solution.py:18
  30.7 20.6 %all-to-all-start.1 = ((s32[64,1,128]{2,1,0:T(1,128)}), s32[64,1,128]{2,1,0:T(1,128)S(1)}, u32[]{:S(2)}, u32[]{:S(2)}) async-start(s32[64,1,128]{2,1,0:T(1,128)} %bitcast.3), calls=%async_computation.1 | async-start | bytes 65536 | tf_op jit(solution)/shard_map/all_to_all | solution.py:93
  51.3 18.0 %all-to-all-start.2 = ((s32[64,1,128]{2,1,0:T(1,128)}), s32[64,1,128]{2,1,0:T(1,128)S(1)}, u32[]{:S(2)}, u32[]{:S(2)}) async-start(s32[64,1,128]{2,1,0:T(1,128)} %bitcast.5), calls=%async_computation.2 | async-start | bytes 65536 | tf_op jit(solution)/shard_map/all_to_all | solution.py:94
  228.4 2.8 copy-start
  527.4 5.6 %copy-start.1 = (s32[1,1,64]{2,1,0:T(1,128)S(1)}, s32[1,1,64]{2,1,0:T(1,128)}, u32[]{:S(2)}) copy-start(s32[1,1,64]{2,1,0:T(1,128)} %param.11) | copy-start | bytes 772
  528.1 18.1 %all-to-all-start.3 = ((f32[6,64,128]{2,0,1:T(8,128)}), f32[6,64,128]{2,0,1:T(8,128)S(1)}, u32[]{:S(2)}, u32[]{:S(2)}) async-start(f32[6,64,128]{2,0,1:T(8,128)} %add_multiply_fusion), calls=%async_computation.3 | async-start | bytes 524288 | tf_op jit(solution)/shard_map/all_to_all | solution.py:97
where the time goes:
time: 552 us; the launch traced here: 547 us
  local copies, waits for them, and re-layouts  305 us (55%)
  other arithmetic  162 us (29%)
  starting transfers between devices  48.1 us (9%)
  waiting for transfers between devices  31.7 us (6%)
    add x15, other arithmetic, sweep_axis(): summed + weights[k] * lax.slice_in_dim(padded, k, k + length, axis=axis)  142 us
    gather x1, local copies, waits for them, and re-layouts, look_up(): jnp.take(flat_tensor, next_cell.reshape(-1), axis=1)  119 us
    gather x1, local copies, waits for them, and re-layouts, look_up(): jnp.take(flat_tensor, here_cell.reshape(-1), axis=1)  119 us
    another operation x8, local copies, waits for them, and re-layouts, tensor_fields(): return jnp.stack(results)  49.1 us
    all_to_all x1, waiting for transfers between devices, body(): lax.all_to_all(served, 'yz', split_axis=1, concat_axis=1, tiled=True)  13.2 us
    all_to_all x1, starting transfers between devices, body(): lax.all_to_all(slot_bins, 'yz', split_axis=0, concat_axis=0, tiled=True)  12.4 us
    all_to_all x1, starting transfers between devices, body(): lax.all_to_all(slot_cells, 'yz', split_axis=0, concat_axis=0, tiled=True)  11.3 us
  transfers between devices with their start and end apart: 8, of which 3 were waited for; matrix products, arithmetic and copies ran while one was open for 1% of the time, Pallas kernels for 0%

commit v1 on v0

v1 whole, which is shorter than its diff:
```python
import functools

import jax
import jax.numpy as jnp
import ml_dtypes
import numpy as np
from jax import lax
from jax.experimental import pallas as pl
from jax.experimental.pallas import tpu as pltpu
from jax.sharding import PartitionSpec as P

HALO = 6
BINS = 8
SIGMA = HALO / 3.0
OFF = 32
MESH = pl.DeviceIdType.MESH
CHUNKS = 4
KROWS = 416
KALL = 2560
PARTS = (0, 1, 2, 0, 1, 0)
WEIGHT_PARTS = (0, 0, 0, 1, 1, 2)
ORDER = (0, 1, 5, 2, 3, 4)
GROUPS = ((0, 192, 0), (192, 320, 1), (320, 384, 2))


def filters():
    k = np.arange(-HALO, HALO + 1).astype(np.float64)
    w0 = np.exp(-k * k / (2.0 * SIGMA * SIGMA))
    w0 = w0 / w0.sum()
    return w0, k / SIGMA**2 * w0, (k * k / SIGMA**4 - 1.0 / SIGMA**2) * w0


def split3(a):
    parts = []
    for _ in range(3):
        p = a.astype(ml_dtypes.bfloat16)
        parts.append(p)
        a = a - p.astype(np.float64)
    return parts


def plane_weights():
    w = filters()
    rows = [(x, y) for x in range(8) for y in range(8)]
    rows += [(x, y) for x in range(-6, 0) for y in range(8)]
    rows += [(x, y) for x in range(8, 14) for y in range(8)]
    rows += [(x, y) for x in range(8) for y in range(-6, 0)]
    rows += [(x, y) for x in range(8) for y in range(8, 14)]
    outer = list(range(-6, 0)) + list(range(8, 14))
    for ys in (range(-6, 0), range(8, 14)):
        rows += [(x, y) for x in outer for y in ys] + [None] * 8
    pairs = ((2, 0), (0, 2), (1, 1), (1, 0), (0, 1), (0, 0))
    a = np.zeros((6, 8, 8, KROWS))
    for k, at in enumerate(rows):
        if at is None:
            continue
        for xo in range(8):
            dx = at[0] - xo + HALO
            for yo in range(8):
                dy = at[1] - yo + HALO
                if 0 <= dx <= 2 * HALO and 0 <= dy <= 2 * HALO:
                    for c, (fx, fy) in enumerate(pairs):
                        a[c, xo, yo, k] = w[fx][dx] * w[fy][dy]
    parts = split3(a.reshape(384, KROWS))
    out = np.zeros((384, KALL), ml_dtypes.bfloat16)
    for i, p in enumerate(WEIGHT_PARTS):
        out[:, i * KROWS : (i + 1) * KROWS] = parts[p]
    return out


def band_weights():
    w = filters()
    out = np.zeros((3, 6 * 256, 256), ml_dtypes.bfloat16)
    for f in range(3):
        band = np.zeros((256, 256))
        for half in range(2):
            for lane in range(128):
                for tap in range(2 * HALO + 1):
                    band[half * 64 + OFF + lane + tap - HALO, half * 128 + lane] = w[f][tap]
        parts = split3(band)
        for i, p in enumerate(WEIGHT_PARTS):
            out[f, i * 256 : (i + 1) * 256] = parts[p]
    return out


def kernel(
    n_gx, n_yz, pot, cells, zeds, bins, plane_hbm, band_hbm, out,
    msg, slots, xb, xa, up, down, cup, cdown, yb, ya, cb, ca,
    plane_w, band_w, pall, gpart, tab, wrow, addr_v, addr_s, served, returned,
    local_sem, slot_send, slot_recv, x_send, x_recv, y_send, y_recv, c_send, c_recv, ret_send, ret_recv,
):
    g = lax.axis_index("gx")
    t = lax.axis_index("yz")
    zc = pot.shape[2] // CHUNKS
    g_up, g_down = lax.rem(g + 1, n_gx), lax.rem(g + n_gx - 1, n_gx)
    t_up, t_down = lax.rem(t + 1, n_yz), lax.rem(t + n_yz - 1, n_yz)

    barrier = pltpu.get_barrier_semaphore()

    @pl.loop(1, n_yz)
    def _(i):
        pl.semaphore_signal(barrier, inc=1, device_id=(g, lax.rem(t + i, n_yz)), device_id_type=MESH)

    for other in (g_up, g_down):
        pl.semaphore_signal(barrier, inc=1, device_id=(other, t), device_id_type=MESH)

    plane_in = pltpu.make_async_copy(plane_hbm, plane_w, local_sem.at[0])
    band_in = pltpu.make_async_copy(band_hbm, band_w, local_sem.at[1])
    plane_in.start()
    band_in.start()
    for i, ref in enumerate((cells, zeds, bins)):
        msg[:, i, :] = ref[...]
    for p in range(8):
        up[6 * p : 6 * p + 6, :] = pot[p, 2:8, :]
        down[6 * p : 6 * p + 6, :] = pot[p, 0:6, :]
    pl.semaphore_wait(barrier, n_yz + 1)

    def remote(src, dst, send, recv, to):
        return pltpu.make_async_remote_copy(
            src_ref=src, dst_ref=dst, send_sem=send, recv_sem=recv, device_id=to, device_id_type=MESH
        )

    x_copies, y_copies, c_copies = [], [], []
    for c in range(CHUNKS):
        zs = pl.ds(c * zc, zc)
        x_copies.append((
            remote(pot.at[pl.ds(2, 6), :, zs], xb.at[:, :, zs], x_send.at[0, c], x_recv.at[0, c], (g_up, t)),
            remote(pot.at[pl.ds(0, 6), :, zs], xa.at[:, :, zs], x_send.at[1, c], x_recv.at[1, c], (g_down, t)),
        ))
        y_copies.append((
            remote(up.at[:, zs], yb.at[:, zs], y_send.at[0, c], y_recv.at[0, c], (g, t_up)),
            remote(down.at[:, zs], ya.at[:, zs], y_send.at[1, c], y_recv.at[1, c], (g, t_down)),
        ))
        c_copies.append((
            remote(cup.at[:, zs], cb.at[:, zs], c_send.at[0, c], c_recv.at[0, c], (g, t_up)),
            remote(cdown.at[:, zs], ca.at[:, zs], c_send.at[1, c], c_recv.at[1, c], (g, t_down)),
        ))
    for copy in x_copies[0] + y_copies[0]:
        copy.start()

    @pl.loop(1, n_yz)
    def _(i):
        to = lax.rem(t + i, n_yz)
        remote(msg.at[to], slots.at[t], slot_send, slot_recv, (g, to)).start()

    own = pltpu.make_async_copy(msg.at[t], slots.at[t], slot_recv)
    own.start()
    for c in range(1, CHUNKS):
        for copy in x_copies[c] + y_copies[c]:
            copy.start()

    pltpu.make_async_copy(msg, slots, slot_recv).wait()
    zr = jnp.bitwise_and(slots[:, 1, :] - OFF, 2047)
    addr_v[...] = slots[:, 0, :] * 32 + jnp.right_shift(zr, 6)
    to_scalar = pltpu.make_async_copy(addr_v, addr_s, local_sem.at[2])
    to_scalar.start()
    zl = jnp.bitwise_and(zr, 63).astype(jnp.float32)
    weight = (slots[:, 2, :].astype(jnp.float32) + 0.5) / BINS
    lane = lax.broadcasted_iota(jnp.int32, (128, 128), 1).astype(jnp.float32)
    columns = jnp.transpose(jnp.concatenate([zl, weight], axis=0))

    def interpolation_rows(homes):
        scale = SIGMA * SIGMA
        for h in homes:
            z_at = columns[:, h : h + 1]
            w_at = columns[:, 64 + h : 65 + h] * scale
            wrow[h] = jnp.where(lane == z_at, scale - w_at, jnp.where(lane == z_at + 1.0, w_at, 0.0))

    def corners(c):
        zs = pl.ds(c * zc, zc)
        for copy in x_copies[c]:
            copy.wait_recv()
        for side, ref, live in ((0, xb, g > 0), (1, xa, g < n_gx - 1)):
            @pl.when(jnp.logical_not(live))
            def _():
                ref[:, :, zs] = jnp.zeros((6, 8, zc), jnp.float32)

            for q in range(6):
                at = 36 * side + 6 * q
                cup[at : at + 6, zs] = ref[q, 2:8, zs]
                cdown[at : at + 6, zs] = ref[q, 0:6, zs]
        for copy in c_copies[c]:
            copy.start()

    step = 64 // CHUNKS
    for c in range(CHUNKS):
        corners(c)
        interpolation_rows(range(c * step, (c + 1) * step))

    pall[6 * KROWS :, :] = jnp.zeros((KALL - 6 * KROWS, zc), jnp.bfloat16)

    def place(at, x):
        rows = x.shape[0]
        p1 = x.astype(jnp.bfloat16)
        r = x - p1.astype(jnp.float32)
        p2 = r.astype(jnp.bfloat16)
        p3 = (r - p2.astype(jnp.float32)).astype(jnp.bfloat16)
        parts = (p1, p2, p3)
        for i, p in enumerate(PARTS):
            pall[i * KROWS + at : i * KROWS + at + rows, :] = parts[p]

    plane_in.wait()
    band_in.wait()

    flat = tab.reshape(64 * 32 * 8, 128)

    def windows(lo, hi):
        for a, b, f in GROUPS:
            lhs = jnp.concatenate(
                [
                    jnp.concatenate([gpart[p, a:b, 128 * w : 128 * w + 256] for p in PARTS], axis=1)
                    for w in range(lo, hi)
                ],
                axis=0,
            )
            h = jnp.dot(lhs, band_w[f], preferred_element_type=jnp.float32)
            at = 0
            for w in range(lo, hi):
                for comp in range(a // 64, b // 64):
                    for ct in range(8):
                        for half in range(2):
                            v = h[at : at + 8, 128 * half : 128 * half + 128]
                            first = ((8 * ct) * 32 + 2 * w + half) * 8 + comp
                            flat[pl.ds(first, 8, stride=256), :] = v
                        at += 8

    for c in range(CHUNKS):
        zs = pl.ds(c * zc, zc)
        place(0, pot[:, :, zs].reshape(64, zc))
        place(64, xb[:, :, zs].reshape(48, zc))
        place(112, xa[:, :, zs].reshape(48, zc))
        for copy in y_copies[c] + c_copies[c]:
            copy.wait_recv()
        first, last = t > 0, t < n_yz - 1
        place(160, jnp.where(first, yb[:, zs], 0.0))
        place(208, jnp.where(last, ya[:, zs], 0.0))
        zero8 = jnp.zeros((8, zc), jnp.float32)
        place(256, jnp.concatenate([jnp.where(first, cb[:, zs], 0.0), zero8], axis=0))
        place(336, jnp.concatenate([jnp.where(last, ca[:, zs], 0.0), zero8], axis=0))
        field = jnp.dot(plane_w[...], pall[...], preferred_element_type=jnp.float32)
        g1 = field.astype(jnp.bfloat16)
        r = field - g1.astype(jnp.float32)
        g2 = r.astype(jnp.bfloat16)
        g3 = (r - g2.astype(jnp.float32)).astype(jnp.bfloat16)
        for p, part in enumerate((g1, g2, g3)):
            gpart[p, :, c * zc : (c + 1) * zc] = part
            if c == 0:
                gpart[p, :, 2048:2176] = part[:, 0:128]
        lo = 0 if c == 0 else 4 * c - 1
        hi = 4 * c + 3 if c < CHUNKS - 1 else 16
        windows(lo, hi)

    to_scalar.wait()
    lane8 = lax.broadcasted_iota(jnp.int32, (8, 128), 1)

    @pl.loop(0, n_yz // 4)
    def _(i):
        homes = [lax.rem(t + 1 + i * 4 + k, n_yz) for k in range(4)]
        for h in homes:
            acc = jnp.zeros((8, 128), jnp.float32)
            for j in range(128):
                row = addr_s[h, j]
                p = tab[row] * wrow[h, pl.ds(j, 1), :]
                acc = jnp.where(lane8 == j, jnp.sum(p, axis=1, keepdims=True), acc)
            served[h] = acc
        for h in homes:
            @pl.when(h != t)
            def _():
                remote(served.at[h], returned.at[t], ret_send, ret_recv, (g, h)).start()

            @pl.when(h == t)
            def _():
                pltpu.make_async_copy(served.at[h], returned.at[t], ret_recv).start()

    pltpu.make_async_copy(served, returned, ret_recv).wait()
    for a, at in enumerate(ORDER):
        out[a] = returned[:, at, :]
    pltpu.make_async_copy(served.at[pl.ds(0, n_yz - 1)], returned.at[pl.ds(0, n_yz - 1)], ret_send).wait()
    pltpu.make_async_copy(msg.at[pl.ds(0, n_yz - 1)], slots.at[pl.ds(0, n_yz - 1)], slot_send).wait()
    for c in range(CHUNKS):
        for copy in x_copies[c] + y_copies[c] + c_copies[c]:
            copy.wait_send()


def body(n_gx, n_yz, potential, gal_cells, gal_z, gal_bins, gal_counts):
    tiles, cap = gal_cells.shape[2], gal_cells.shape[3]
    cz = potential.shape[2]
    f32, bf16, i32 = jnp.float32, jnp.bfloat16, jnp.int32
    vmem = pl.BlockSpec(memory_space=pltpu.VMEM)
    hbm = pl.BlockSpec(memory_space=pl.ANY)
    dma = pltpu.SemaphoreType.DMA
    returned = pl.pallas_call(
        functools.partial(kernel, n_gx, n_yz),
        out_shape=jax.ShapeDtypeStruct((6, tiles, cap), f32),
        in_specs=[vmem] * 4 + [hbm] * 2,
        out_specs=vmem,
        scratch_shapes=[
            pltpu.VMEM((tiles, 4, cap), i32),
            pltpu.VMEM((tiles, 4, cap), i32),
            pltpu.VMEM((6, 8, cz), f32),
            pltpu.VMEM((6, 8, cz), f32),
            pltpu.VMEM((48, cz), f32),
            pltpu.VMEM((48, cz), f32),
            pltpu.VMEM((72, cz), f32),
            pltpu.VMEM((72, cz), f32),
            pltpu.VMEM((48, cz), f32),
            pltpu.VMEM((48, cz), f32),
            pltpu.VMEM((72, cz), f32),
            pltpu.VMEM((72, cz), f32),
            pltpu.VMEM((384, KALL), bf16),
            pltpu.VMEM((3, 1536, 256), bf16),
            pltpu.VMEM((KALL, cz // CHUNKS), bf16),
            pltpu.VMEM((3, 384, cz + 128), bf16),
            pltpu.VMEM((64 * 32, 8, 128), f32),
            pltpu.VMEM((tiles, cap, 128), f32),
            pltpu.VMEM((tiles, cap), i32),
            pltpu.SMEM((tiles, cap), i32),
            pltpu.VMEM((tiles, 8, cap), f32),
            pltpu.VMEM((tiles, 8, cap), f32),
            dma((3,)),
            dma,
            dma,
            dma((2, CHUNKS)),
            dma((2, CHUNKS)),
            dma((2, CHUNKS)),
            dma((2, CHUNKS)),
            dma((2, CHUNKS)),
            dma((2, CHUNKS)),
            dma,
            dma,
        ],
        compiler_params=pltpu.CompilerParams(
            collective_id=0, has_side_effects=True, vmem_limit_bytes=60 * 1024 * 1024
        ),
        name="tidal",
    )(
        potential,
        gal_cells.reshape(tiles, cap),
        gal_z.reshape(tiles, cap),
        gal_bins.reshape(tiles, cap),
        jnp.asarray(plane_weights()),
        jnp.asarray(band_weights()),
    )
    slot_index = lax.broadcasted_iota(jnp.int32, (tiles, cap), 1)
    live = slot_index < gal_counts.reshape(tiles, 1)
    tidal = jnp.where(live[None], returned, jnp.float32(0.0))
    return tidal.reshape(6, 1, 1, tiles * cap)


def solution(mesh):
    return jax.shard_map(
        functools.partial(body, mesh.shape["gx"], mesh.shape["yz"]),
        mesh=mesh,
        in_specs=(
            P("gx", "yz", None),
            P("gx", "yz", None, None),
            P("gx", "yz", None, None),
            P("gx", "yz", None, None),
            P("gx", "yz", None),
        ),
        out_specs=P(None, "gx", "yz", None),
        check_vma=False,
    )
```

time: 552 us -> 56.6 us (0.10)
  local copies, waits for them, and re-layouts: 305 us -> 0 us
  other arithmetic: 162 us -> 2.35 us
  Pallas kernels: 0 us -> 54.1 us
  starting transfers between devices: 48.1 us -> 0 us
  waiting for transfers between devices: 31.7 us -> 0 us
    gather x2 -> x0, local copies, waits for them, and re-layouts: 237 us -> none  [the longest x1 119 us: look_up(): jnp.take(flat_tensor, next_cell.reshape(-1), axis=1)]
    add x15 -> x0, other arithmetic: 142 us -> none  [sweep_axis(): summed + weights[k] * lax.slice_in_dim(padded, k, k + length, axis=axis)]
    pallas_call x0 -> x1, Pallas kernels: none -> 54.1 us  [body(): pl.pallas_call(functools.partial(kernel, n_gx, n_yz), out_shape=jax.Shape...]
    another operation x8 -> x0, local copies, waits for them, and re-layouts: 49.1 us -> none  [tensor_fields(): return jnp.stack(results)]
    all_to_all x4 -> x0, starting transfers between devices: 37.3 us -> none  [the longest x1 12.4 us: body(): lax.all_to_all(slot_bins, 'yz', split_axis=0, concat_axis=0, tiled=True)]
    all_to_all x4 -> x0, waiting for transfers between devices: 31.7 us -> none  [the longest x1 13.2 us: body(): lax.all_to_all(served, 'yz', split_axis=1, concat_axis=1, tiled=True)]
    select_n x2 -> x1, other arithmetic: 14.9 us -> 1.62 us  [body(): tidal = jnp.where(live[None], returned, jnp.float32(0.0))]
    ppermute x4 -> x0, starting transfers between devices: 10.8 us -> none  [the longest x2 7.59 us: padded_2(): before = lax.ppermute(last, axis, up)]
  transfers between devices with their start and end apart: 8 -> 0, of which waited for: 3 -> 0; matrix products, arithmetic and copies ran while one was open for 1% -> 0% of each run, Pallas kernels for 0% -> 0%
where the time goes in v1:
time: 56.6 us; the launch traced here: 56.4 us
  Pallas kernels  54.1 us (96%)
  other arithmetic  2.35 us (4%)
    pallas_call x1, Pallas kernels, body(): pl.pallas_call(functools.partial(kernel, n_gx, n_yz), out_shape=jax.Shape...  54.1 us
    select_n x1, other arithmetic, body(): tidal = jnp.where(live[None], returned, jnp.float32(0.0))  1.62 us

profile of v1, /device:TPU:1, one launch (start us, length us, event | category | flops | bytes accessed | tf_op | source)
XLA Modules:
  0.0 56.4 jit_solution(2494847538413606609)
XLA Ops:
  0.0 0.7 %iota_compare_fusion = pred[64,128]{1,0:T(8,128)(4,1)S(1)} fusion(s32[64]{0:T(128)} %bitcast.8), kind=kLoop, calls=%fused_computation.1 | loop fusion | flops 8192 | bytes 8448 | tf_op jit(solution)/shard_map/lt | solution.py:345
  0.7 54.1 %tidal.1 = f32[6,64,128]{2,1,0:T(8,128)} custom-call(f32[8,8,2048]{2,1,0:T(8,128)} %pot.1, s32[64,128]{1,0:T(8,128)} %bitcast.5, s32[64,128]{1,0:T(8,128)} %bitcast.6, s32[64,128]{1,0:T(8,128)} %bitcast.7, bf16[384,2560]{1,0:T(8,128)(2,1)} %constant.6.clone.plane_hbm, bf16[3,1536,256]{2,1,0:T(8,128)(2,1)} %constant.7.clone.band_hbm), custom_call_target="tpu_custom_call" | custom-call | tf_op jit(solution)/shard_map/tidal/pallas_call | solution.py:292
  54.8 1.6 %broadcast_select_fusion = f32[6,64,128]{2,1,0:T(8,128)} fusion(f32[6,64,128]{2,1,0:T(8,128)} %tidal.1, pred[64,128]{1,0:T(8,128)(4,1)S(1)} %iota_compare_fusion), kind=kLoop, calls=%fused_computation | loop fusion | flops 49152 | bytes 401408 | tf_op jit(solution)/shard_map/jit(_where)/select_n | solution.py:346

commit v2 on v1

v2 whole, which is shorter than its diff:
```python
import functools

import jax
import jax.numpy as jnp
import ml_dtypes
import numpy as np
from jax import lax
from jax.experimental import pallas as pl
from jax.experimental.pallas import tpu as pltpu
from jax.sharding import PartitionSpec as P

HALO = 6
BINS = 8
SIGMA = HALO / 3.0
STEP = 116
MESH = pl.DeviceIdType.MESH
CHUNKS = 4
PLANE = 8
STRIDE = 1
WINDOWS = 19
FIRST = 160
SECOND = 256
KROWS = FIRST + SECOND
KFIRST, KSECOND = 1024, 6 * SECOND
PARTS = (0, 1, 2, 0, 1, 0)
WEIGHT_PARTS = (0, 0, 0, 1, 1, 2)
ORDER = (0, 1, 5, 2, 3, 4)
GROUPS = ((0, 192, 0), (192, 320, 1), (320, 384, 2))


def filters():
    k = np.arange(-HALO, HALO + 1).astype(np.float64)
    w0 = np.exp(-k * k / (2.0 * SIGMA * SIGMA))
    w0 = w0 / w0.sum()
    return w0, k / SIGMA**2 * w0, (k * k / SIGMA**4 - 1.0 / SIGMA**2) * w0


def split3(a):
    parts = []
    for _ in range(3):
        p = a.astype(ml_dtypes.bfloat16)
        parts.append(p)
        a = a - p.astype(np.float64)
    return parts


def plane_weights():
    w = filters()
    rows = [(x, y) for x in range(8) for y in range(8)]
    rows += [(x, y) for x in range(-6, 0) for y in range(8)]
    rows += [(x, y) for x in range(8, 14) for y in range(8)]
    rows += [(x, y) for x in range(8) for y in range(-6, 0)]
    rows += [(x, y) for x in range(8) for y in range(8, 14)]
    outer = list(range(-6, 0)) + list(range(8, 14))
    for ys in (range(-6, 0), range(8, 14)):
        rows += [(x, y) for x in outer for y in ys] + [None] * 8
    pairs = ((2, 0), (0, 2), (1, 1), (1, 0), (0, 1), (0, 0))
    a = np.zeros((6, 8, 8, KROWS))
    for k, at in enumerate(rows):
        if at is None:
            continue
        for xo in range(8):
            dx = at[0] - xo + HALO
            for yo in range(8):
                dy = at[1] - yo + HALO
                if 0 <= dx <= 2 * HALO and 0 <= dy <= 2 * HALO:
                    for c, (fx, fy) in enumerate(pairs):
                        a[c, xo, yo, k] = w[fx][dx] * w[fy][dy]
    parts = split3(a.reshape(384, KROWS))
    out = np.zeros((384, KFIRST + KSECOND), ml_dtypes.bfloat16)
    for i, p in enumerate(WEIGHT_PARTS):
        out[:, i * FIRST : (i + 1) * FIRST] = parts[p][:, :FIRST]
        at = KFIRST + i * SECOND
        out[:, at : at + SECOND] = parts[p][:, FIRST:]
    return out


def band_weights():
    w = filters()
    out = np.zeros((3, 6 * 256, 256), ml_dtypes.bfloat16)
    for f in range(3):
        band = np.zeros((256, 256))
        for half in range(2):
            for lane in range(128):
                for tap in range(2 * HALO + 1):
                    band[half * STEP + lane + tap, half * 128 + lane] = w[f][tap]
        parts = split3(band)
        for i, p in enumerate(WEIGHT_PARTS):
            out[f, i * 256 : (i + 1) * 256] = parts[p]
    return out


def kernel(
    n_gx, n_yz, pot_hbm, cells_hbm, zeds_hbm, bins_hbm, counts_hbm, plane_hbm, band_hbm, out,
    pot, cells, zeds, bins, counts, msg, slots, xb, xa, up, down, cup, cdown, yb, ya, cb, ca,
    plane_w, band_w, first_in, second_in, partial, tab, wrow, addr_v, addr_s, served, returned, live,
    local_sem, in_sem, ready, slot_send, slot_recv, x_send, x_recv, y_send, y_recv, c_send, c_recv, ret_send, ret_recv,
):
    g = lax.axis_index("gx")
    t = lax.axis_index("yz")
    zc = pot.shape[2] // CHUNKS
    g_up, g_down = lax.rem(g + 1, n_gx), lax.rem(g + n_gx - 1, n_gx)
    t_up, t_down = lax.rem(t + 1, n_yz), lax.rem(t + n_yz - 1, n_yz)

    barrier = pltpu.get_barrier_semaphore()

    z, q = t // PLANE, lax.rem(t, PLANE)
    lines = n_yz // PLANE
    in_plane = [(g, z * PLANE + lax.rem(q + i, PLANE)) for i in range(1, PLANE)]
    in_line = [(g, lax.rem(z + i, lines) * PLANE + q) for i in range(1, lines)]
    for to in [(g_up, t), (g_down, t)] + in_plane + in_line:
        pl.semaphore_signal(barrier, inc=1, device_id=to, device_id_type=MESH)

    @pl.when(q == PLANE - 1)
    def _():
        pl.semaphore_signal(barrier, inc=1, device_id=(g, t_up), device_id_type=MESH)

    @pl.when(q == 0)
    def _():
        pl.semaphore_signal(barrier, inc=1, device_id=(g, t_down), device_id_type=MESH)

    loads = [
        pltpu.make_async_copy(src, dst, in_sem.at[i])
        for i, (src, dst) in enumerate(
            ((pot_hbm, pot), (cells_hbm, cells), (zeds_hbm, zeds), (bins_hbm, bins), (counts_hbm, counts))
        )
    ]
    for load in loads:
        load.start()
    plane_in = pltpu.make_async_copy(plane_hbm, plane_w, local_sem.at[0])
    band_in = pltpu.make_async_copy(band_hbm, band_w, local_sem.at[1])
    plane_in.start()
    band_in.start()
    for load in loads:
        load.wait()
    for i, ref in enumerate((cells, zeds, bins)):
        msg[:, i, :] = ref[...]
    for p in range(8):
        up[6 * p : 6 * p + 6, :] = pot[p, 2:8, :]
        down[6 * p : 6 * p + 6, :] = pot[p, 0:6, :]
    edge = jnp.logical_or(q == PLANE - 1, q == 0)

    @pl.when(edge)
    def _():
        pl.semaphore_wait(barrier, PLANE + lines + 1)

    @pl.when(jnp.logical_not(edge))
    def _():
        pl.semaphore_wait(barrier, PLANE + lines)

    def remote(src, dst, send, recv, to):
        return pltpu.make_async_remote_copy(
            src_ref=src, dst_ref=dst, send_sem=send, recv_sem=recv, device_id=to, device_id_type=MESH
        )

    x_copies, y_copies, c_copies = [], [], []
    for c in range(CHUNKS):
        zs = pl.ds(c * zc, zc)
        x_copies.append((
            remote(pot.at[pl.ds(2, 6), :, zs], xb.at[:, :, zs], x_send.at[0, c], x_recv.at[0, c], (g_up, t)),
            remote(pot.at[pl.ds(0, 6), :, zs], xa.at[:, :, zs], x_send.at[1, c], x_recv.at[1, c], (g_down, t)),
        ))
        y_copies.append((
            remote(up.at[:, zs], yb.at[:, zs], y_send.at[0, c], y_recv.at[0, c], (g, t_up)),
            remote(down.at[:, zs], ya.at[:, zs], y_send.at[1, c], y_recv.at[1, c], (g, t_down)),
        ))
        c_copies.append((
            remote(cup.at[:, zs], cb.at[:, zs], c_send.at[0, c], c_recv.at[0, c], (g, t_up)),
            remote(cdown.at[:, zs], ca.at[:, zs], c_send.at[1, c], c_recv.at[1, c], (g, t_down)),
        ))
    for copy in x_copies[0]:
        copy.start()
    for c in range(CHUNKS):
        for copy in y_copies[c]:
            copy.start()
    for copy in x_copies[0]:
        copy.wait_send()
    for copy in x_copies[1] + x_copies[2]:
        copy.start()
    for to in in_plane:
        pl.semaphore_signal(ready, inc=1, device_id=to, device_id_type=MESH)
    pl.semaphore_wait(ready, PLANE - 1)

    @pl.loop(1, n_yz)
    def _(i):
        to = lax.rem(t + i * STRIDE, n_yz)
        remote(msg.at[to], slots.at[t], slot_send, slot_recv, (g, to)).start()

    pltpu.make_async_copy(msg.at[t], slots.at[t], slot_recv).start()
    for copy in x_copies[3]:
        copy.start()

    def corners(c):
        zs = pl.ds(c * zc, zc)
        for copy in x_copies[c]:
            copy.wait_recv()
        for side, ref, live in ((0, xb, g > 0), (1, xa, g < n_gx - 1)):
            @pl.when(jnp.logical_not(live))
            def _():
                ref[:, :, zs] = jnp.zeros((6, 8, zc), jnp.float32)

            for q in range(6):
                at = 36 * side + 6 * q
                cup[at : at + 6, zs] = ref[q, 2:8, zs]
                cdown[at : at + 6, zs] = ref[q, 0:6, zs]
        for copy in c_copies[c]:
            copy.start()

    def split(x):
        p1 = x.astype(jnp.bfloat16)
        r = x - p1.astype(jnp.float32)
        p2 = r.astype(jnp.bfloat16)
        return p1, p2, (r - p2.astype(jnp.float32)).astype(jnp.bfloat16)

    def place(ref, size, at, x):
        rows = x.shape[0]
        parts = split(x)
        for i, p in enumerate(PARTS):
            ref[i * size + at : i * size + at + rows, :] = parts[p]

    def first_part(c):
        zs = pl.ds(c * zc, zc)
        place(first_in, FIRST, 0, pot[:, :, zs].reshape(64, zc))
        place(first_in, FIRST, 64, xb[:, :, zs].reshape(48, zc))
        place(first_in, FIRST, 112, xa[:, :, zs].reshape(48, zc))
        partial[:, zs] = jnp.dot(plane_w[:, :KFIRST], first_in[...], preferred_element_type=jnp.float32)

    first_in[6 * FIRST :, :] = jnp.zeros((KFIRST - 6 * FIRST, zc), jnp.bfloat16)
    plane_in.wait()
    band_in.wait()
    for c in range(CHUNKS):
        corners(c)
        first_part(c)

    pltpu.make_async_copy(msg, slots, slot_recv).wait()
    zr = jnp.bitwise_and(slots[:, 1, :] - HALO, 2047)
    window = jnp.right_shift(zr * 565, 16)
    addr_v[...] = slots[:, 0, :] * WINDOWS + window
    to_scalar = pltpu.make_async_copy(addr_v, addr_s, local_sem.at[2])
    to_scalar.start()
    zl = (zr - window * STEP).astype(jnp.float32)
    weight = (slots[:, 2, :].astype(jnp.float32) + 0.5) / BINS
    lane = lax.broadcasted_iota(jnp.int32, (128, 128), 1).astype(jnp.float32)
    columns = jnp.transpose(jnp.concatenate([zl, weight], axis=0))

    def interpolation_rows(homes):
        scale = SIGMA * SIGMA
        for h in homes:
            z_at = columns[:, h : h + 1]
            w_at = columns[:, 64 + h : 65 + h] * scale
            wrow[h] = jnp.where(lane == z_at, scale - w_at, jnp.where(lane == z_at + 1.0, w_at, 0.0))


    flat = tab.reshape(64 * WINDOWS * 8, 128)

    def windows(lo, hi):
        parts = [split(partial[:, 2 * STEP * w : 2 * STEP * w + 256]) for w in range(lo, hi)]
        for a, b, f in GROUPS:
            lhs = jnp.concatenate([jnp.concatenate([g[p][a:b] for p in PARTS], axis=1) for g in parts], axis=0)
            h = jnp.dot(lhs, band_w[f], preferred_element_type=jnp.float32)
            at = 0
            for w in range(lo, hi):
                for comp in range(a // 64, b // 64):
                    for ct in range(8):
                        for half in range(2):
                            v = h[at : at + 8, 128 * half : 128 * half + 128]
                            first = ((8 * ct) * WINDOWS + 2 * w + half) * 8 + comp
                            flat[pl.ds(first, 8, stride=8 * WINDOWS), :] = v
                        at += 8

    def dense(c):
        zs = pl.ds(c * zc, zc)
        for copy in y_copies[c] + c_copies[c]:
            copy.wait_recv()
        first, last = t > 0, t < n_yz - 1
        place(second_in, SECOND, 0, jnp.where(first, yb[:, zs], 0.0))
        place(second_in, SECOND, 48, jnp.where(last, ya[:, zs], 0.0))
        zero8 = jnp.zeros((8, zc), jnp.float32)
        place(second_in, SECOND, 96, jnp.concatenate([jnp.where(first, cb[:, zs], 0.0), zero8], axis=0))
        place(second_in, SECOND, 176, jnp.concatenate([jnp.where(last, ca[:, zs], 0.0), zero8], axis=0))
        field = partial[:, zs] + jnp.dot(plane_w[:, KFIRST:], second_in[...], preferred_element_type=jnp.float32)
        partial[:, zs] = field
        if c == 0:
            partial[:, 2048:2176] = field[:, 0:128]
        lo, hi = 2 * c, 2 * c + (2 if c < CHUNKS - 1 else 3)
        windows(lo, hi)

    interpolation_rows(range(n_yz))
    live[...] = jnp.transpose(jnp.broadcast_to(counts[...], (128, n_yz)))
    for c in range(CHUNKS):
        dense(c)
    to_scalar.wait()
    lane8 = lax.broadcasted_iota(jnp.int32, (8, 128), 1)

    six = pl.ds(0, 6)

    def serve(h):
        acc = jnp.zeros((8, 128), jnp.float32)
        for j in range(128):
            row = addr_s[h, j]
            p = tab[row] * wrow[h, pl.ds(j, 1), :]
            acc = jnp.where(lane8 == j, jnp.sum(p, axis=1, keepdims=True), acc)
        served[h] = acc

    @pl.loop(0, lines)
    def _(i):
        away = lines // 2 + (i + 1) // 2 * (1 - 2 * lax.rem(i, 2))
        homes = [lax.rem(z + away, lines) * PLANE + lax.rem(q + 1 + k, PLANE) for k in range(PLANE)]
        for h in homes:
            serve(h)
        for h in homes:
            @pl.when(h != t)
            def _():
                remote(served.at[h, six], returned.at[t, six], ret_send, ret_recv, (g, h)).start()

            @pl.when(h == t)
            def _():
                pltpu.make_async_copy(served.at[t, six], returned.at[t, six], ret_recv).start()

    pltpu.make_async_copy(served.at[:, six], returned.at[:, six], ret_recv).wait()
    keep = lax.broadcasted_iota(jnp.int32, (n_yz, 128), 1) < live[...]
    for a, at in enumerate(ORDER):
        out[a] = jnp.where(keep, returned[:, at, :], 0.0)
    others = pl.ds(0, n_yz - 1)
    pltpu.make_async_copy(served.at[others, six], returned.at[others, six], ret_send).wait()
    pltpu.make_async_copy(msg.at[pl.ds(0, n_yz - 1)], slots.at[pl.ds(0, n_yz - 1)], slot_send).wait()
    for c in range(CHUNKS):
        for copy in (x_copies[c] if c else ()) + y_copies[c] + c_copies[c]:
            copy.wait_send()


def body(n_gx, n_yz, potential, gal_cells, gal_z, gal_bins, gal_counts):
    tiles, cap = gal_cells.shape[2], gal_cells.shape[3]
    cz = potential.shape[2]
    f32, bf16, i32 = jnp.float32, jnp.bfloat16, jnp.int32
    vmem = pl.BlockSpec(memory_space=pltpu.VMEM)
    hbm = pl.BlockSpec(memory_space=pl.ANY)
    dma = pltpu.SemaphoreType.DMA
    returned = pl.pallas_call(
        functools.partial(kernel, n_gx, n_yz),
        out_shape=jax.ShapeDtypeStruct((6, tiles, cap), f32),
        in_specs=[hbm] * 7,
        out_specs=vmem,
        scratch_shapes=[
            pltpu.VMEM(potential.shape, f32),
            pltpu.VMEM((tiles, cap), i32),
            pltpu.VMEM((tiles, cap), i32),
            pltpu.VMEM((tiles, cap), i32),
            pltpu.VMEM((1, tiles), i32),
            pltpu.VMEM((tiles, 4, cap), i32),
            pltpu.VMEM((tiles, 4, cap), i32),
            pltpu.VMEM((6, 8, cz), f32),
            pltpu.VMEM((6, 8, cz), f32),
            pltpu.VMEM((48, cz), f32),
            pltpu.VMEM((48, cz), f32),
            pltpu.VMEM((72, cz), f32),
            pltpu.VMEM((72, cz), f32),
            pltpu.VMEM((48, cz), f32),
            pltpu.VMEM((48, cz), f32),
            pltpu.VMEM((72, cz), f32),
            pltpu.VMEM((72, cz), f32),
            pltpu.VMEM((384, KFIRST + KSECOND), bf16),
            pltpu.VMEM((3, 1536, 256), bf16),
            pltpu.VMEM((KFIRST, cz // CHUNKS), bf16),
            pltpu.VMEM((KSECOND, cz // CHUNKS), bf16),
            pltpu.VMEM((384, cz + 128), f32),
            pltpu.VMEM((64 * WINDOWS, 8, 128), f32),
            pltpu.VMEM((tiles, cap, 128), f32),
            pltpu.VMEM((tiles, cap), i32),
            pltpu.SMEM((tiles, cap), i32),
            pltpu.VMEM((tiles, 8, cap), f32),
            pltpu.VMEM((tiles, 8, cap), f32),
            pltpu.VMEM((tiles, cap), i32),
            dma((3,)),
            dma((5,)),
            pltpu.SemaphoreType.REGULAR,
            dma,
            dma,
            dma((2, CHUNKS)),
            dma((2, CHUNKS)),
            dma((2, CHUNKS)),
            dma((2, CHUNKS)),
            dma((2, CHUNKS)),
            dma((2, CHUNKS)),
            dma,
            dma,
        ],
        compiler_params=pltpu.CompilerParams(
            collective_id=0, has_side_effects=True, vmem_limit_bytes=60 * 1024 * 1024
        ),
        name="tidal",
    )(
        potential,
        gal_cells.reshape(tiles, cap),
        gal_z.reshape(tiles, cap),
        gal_bins.reshape(tiles, cap),
        gal_counts.reshape(1, tiles),
        jnp.asarray(plane_weights()),
        jnp.asarray(band_weights()),
    )
    return returned.reshape(6, 1, 1, tiles * cap)


def solution(mesh):
    return jax.shard_map(
        functools.partial(body, mesh.shape["gx"], mesh.shape["yz"]),
        mesh=mesh,
        in_specs=(
            P("gx", "yz", None),
            P("gx", "yz", None, None),
            P("gx", "yz", None, None),
            P("gx", "yz", None, None),
            P("gx", "yz", None),
        ),
        out_specs=P(None, "gx", "yz", None),
        check_vma=False,
    )
```

time: 56.6 us -> 51.1 us (0.903)
  Pallas kernels: 54.1 us -> 49.4 us
  other arithmetic: 2.35 us -> 0 us
  local copies, waits for them, and re-layouts: 0 us -> 1.62 us
    pallas_call x1, Pallas kernels: 54.1 us -> 49.4 us  [body(): pl.pallas_call(functools.partial(kernel, n_gx, n_yz), out_shape=jax.Shape...]
    select_n x1 -> x0, other arithmetic: 1.62 us -> none  [body(): tidal = jnp.where(live[None], returned, jnp.float32(0.0))]
    unnamed x0 -> x1, local copies, waits for them, and re-layouts: none -> 1.62 us
    lt x1 -> x0, other arithmetic: 0.73 us -> none  [body(): live = slot_index < gal_counts.reshape(tiles, 1)]
where the time goes in v2:
time: 51.1 us; the launch traced here: 51 us
  Pallas kernels  49.4 us (97%)
  local copies, waits for them, and re-layouts  1.62 us (3%)
    pallas_call x1, Pallas kernels, body(): pl.pallas_call(functools.partial(kernel, n_gx, n_yz), out_shape=jax.Shape...  49.4 us
    unnamed x1, local copies, waits for them, and re-layouts  1.62 us

profile of v2, /device:TPU:1, one launch (start us, length us, event | category | flops | bytes accessed | tf_op | source)
XLA Modules:
  0.0 51.0 jit_solution(659520667037669808)
XLA Ops:
  0.0 49.4 %tidal.1 = f32[6,64,128]{2,1,0:T(8,128)} custom-call(f32[8,8,2048]{2,1,0:T(8,128)} %pot_hbm.1, s32[64,128]{1,0:T(8,128)} %bitcast.6, s32[64,128]{1,0:T(8,128)} %bitcast.7, s32[64,128]{1,0:T(8,128)} %bitcast.8, s32[1,64]{1,0:T(1,128)} %bitcast.9, bf16[384,2560]{1,0:T(8,128)(2,1)} %constant.4.clone.plane_hbm, bf16[3,1536,256]{2,1,0:T(8,128)(2,1)} %constant.5.clone.band_hbm), custom_call_target="tpu_custom_call" | custom-call | tf_op jit(solution)/shard_map/tidal/pallas_call | solution.py:339
  49.4 1.6 %copy.11 = f32[6,1,1,8192]{3,2,1,0:T(1,128)} copy(f32[6,1,1,8192]{3,2,1,0:T(1,128)} %bitcast.5) | data formatting | bytes 393216

commit v3 on v2

--- a/solution.py
+++ b/solution.py
@@ -228,7 +228,7 @@
     first_in[6 * FIRST :, :] = jnp.zeros((KFIRST - 6 * FIRST, zc), jnp.bfloat16)
     plane_in.wait()
     band_in.wait()
-    for c in range(CHUNKS):
+    for c in range(CHUNKS - 1):
         corners(c)
         first_part(c)
 
@@ -250,7 +250,9 @@
             w_at = columns[:, 64 + h : 65 + h] * scale
             wrow[h] = jnp.where(lane == z_at, scale - w_at, jnp.where(lane == z_at + 1.0, w_at, 0.0))
 
-
+    interpolation_rows(range(n_yz // 2))
+    corners(3)
+    first_part(3)
     flat = tab.reshape(64 * WINDOWS * 8, 128)
 
     def windows(lo, hi):
@@ -285,7 +287,7 @@
         lo, hi = 2 * c, 2 * c + (2 if c < CHUNKS - 1 else 3)
         windows(lo, hi)
 
-    interpolation_rows(range(n_yz))
+    interpolation_rows(range(n_yz // 2, n_yz))
     live[...] = jnp.transpose(jnp.broadcast_to(counts[...], (128, n_yz)))
     for c in range(CHUNKS):
         dense(c)
@@ -302,20 +304,20 @@
             acc = jnp.where(lane8 == j, jnp.sum(p, axis=1, keepdims=True), acc)
         served[h] = acc
 
-    @pl.loop(0, lines)
-    def _(i):
+    def serve_line(i, count):
         away = lines // 2 + (i + 1) // 2 * (1 - 2 * lax.rem(i, 2))
         homes = [lax.rem(z + away, lines) * PLANE + lax.rem(q + 1 + k, PLANE) for k in range(PLANE)]
         for h in homes:
             serve(h)
-        for h in homes:
-            @pl.when(h != t)
-            def _():
-                remote(served.at[h, six], returned.at[t, six], ret_send, ret_recv, (g, h)).start()
-
-            @pl.when(h == t)
-            def _():
-                pltpu.make_async_copy(served.at[t, six], returned.at[t, six], ret_recv).start()
+        for h in homes[:count]:
+            remote(served.at[h, six], returned.at[t, six], ret_send, ret_recv, (g, h)).start()
+
+    @pl.loop(0, lines - 1)
+    def _(i):
+        serve_line(i, PLANE)
+
+    serve_line(lines - 1, PLANE - 1)
+    pltpu.make_async_copy(served.at[t, six], returned.at[t, six], ret_recv).start()
 
     pltpu.make_async_copy(served.at[:, six], returned.at[:, six], ret_recv).wait()
     keep = lax.broadcasted_iota(jnp.int32, (n_yz, 128), 1) < live[...]

time: 51.1 us -> 49.9 us (0.977)
  Pallas kernels: 49.4 us -> 48.2 us
    pallas_call x1, Pallas kernels: 49.4 us -> 48.2 us  [body(): pl.pallas_call(functools.partial(kernel, n_gx, n_yz), out_shape=jax.Shape...]
where the time goes in v3:
time: 49.9 us; the launch traced here: 49.8 us
  Pallas kernels  48.2 us (97%)
  local copies, waits for them, and re-layouts  1.62 us (3%)
    pallas_call x1, Pallas kernels, body(): pl.pallas_call(functools.partial(kernel, n_gx, n_yz), out_shape=jax.Shape...  48.2 us
    unnamed x1, local copies, waits for them, and re-layouts  1.62 us

profile of v3, /device:TPU:1, one launch (start us, length us, event | category | flops | bytes accessed | tf_op | source)
XLA Modules:
  0.0 49.8 jit_solution(1942267343934774178)
XLA Ops:
  0.0 48.2 %tidal.1 = f32[6,64,128]{2,1,0:T(8,128)} custom-call(f32[8,8,2048]{2,1,0:T(8,128)} %pot_hbm.1, s32[64,128]{1,0:T(8,128)} %bitcast.6, s32[64,128]{1,0:T(8,128)} %bitcast.7, s32[64,128]{1,0:T(8,128)} %bitcast.8, s32[1,64]{1,0:T(1,128)} %bitcast.9, bf16[384,2560]{1,0:T(8,128)(2,1)} %constant.4.clone.plane_hbm, bf16[3,1536,256]{2,1,0:T(8,128)(2,1)} %constant.5.clone.band_hbm), custom_call_target="tpu_custom_call" | custom-call | tf_op jit(solution)/shard_map/tidal/pallas_call | solution.py:341
  48.2 1.6 %copy.11 = f32[6,1,1,8192]{3,2,1,0:T(1,128)} copy(f32[6,1,1,8192]{3,2,1,0:T(1,128)} %bitcast.5) | data formatting | bytes 393216

commit v4 on v3

--- a/solution.py
+++ b/solution.py
@@ -18,10 +18,10 @@
 PLANE = 8
 STRIDE = 1
 WINDOWS = 19
-FIRST = 160
-SECOND = 256
+FIRST = 256
+SECOND = 160
 KROWS = FIRST + SECOND
-KFIRST, KSECOND = 1024, 6 * SECOND
+KFIRST, KSECOND = 6 * FIRST, 1024
 PARTS = (0, 1, 2, 0, 1, 0)
 WEIGHT_PARTS = (0, 0, 0, 1, 1, 2)
 ORDER = (0, 1, 5, 2, 3, 4)
@@ -223,9 +223,13 @@
         place(first_in, FIRST, 0, pot[:, :, zs].reshape(64, zc))
         place(first_in, FIRST, 64, xb[:, :, zs].reshape(48, zc))
         place(first_in, FIRST, 112, xa[:, :, zs].reshape(48, zc))
+        for copy in y_copies[c]:
+            copy.wait_recv()
+        place(first_in, FIRST, 160, jnp.where(t > 0, yb[:, zs], 0.0))
+        place(first_in, FIRST, 208, jnp.where(t < n_yz - 1, ya[:, zs], 0.0))
         partial[:, zs] = jnp.dot(plane_w[:, :KFIRST], first_in[...], preferred_element_type=jnp.float32)
 
-    first_in[6 * FIRST :, :] = jnp.zeros((KFIRST - 6 * FIRST, zc), jnp.bfloat16)
+    second_in[6 * SECOND :, :] = jnp.zeros((KSECOND - 6 * SECOND, zc), jnp.bfloat16)
     plane_in.wait()
     band_in.wait()
     for c in range(CHUNKS - 1):
@@ -272,14 +276,12 @@
 
     def dense(c):
         zs = pl.ds(c * zc, zc)
-        for copy in y_copies[c] + c_copies[c]:
+        for copy in c_copies[c]:
             copy.wait_recv()
         first, last = t > 0, t < n_yz - 1
-        place(second_in, SECOND, 0, jnp.where(first, yb[:, zs], 0.0))
-        place(second_in, SECOND, 48, jnp.where(last, ya[:, zs], 0.0))
         zero8 = jnp.zeros((8, zc), jnp.float32)
-        place(second_in, SECOND, 96, jnp.concatenate([jnp.where(first, cb[:, zs], 0.0), zero8], axis=0))
-        place(second_in, SECOND, 176, jnp.concatenate([jnp.where(last, ca[:, zs], 0.0), zero8], axis=0))
+        place(second_in, SECOND, 0, jnp.concatenate([jnp.where(first, cb[:, zs], 0.0), zero8], axis=0))
+        place(second_in, SECOND, 80, jnp.concatenate([jnp.where(last, ca[:, zs], 0.0), zero8], axis=0))
         field = partial[:, zs] + jnp.dot(plane_w[:, KFIRST:], second_in[...], preferred_element_type=jnp.float32)
         partial[:, zs] = field
         if c == 0:
@@ -287,10 +289,11 @@
         lo, hi = 2 * c, 2 * c + (2 if c < CHUNKS - 1 else 3)
         windows(lo, hi)
 
+    live[...] = jnp.transpose(jnp.broadcast_to(counts[...], (128, n_yz)))
+    for c in range(CHUNKS - 1):
+        dense(c)
     interpolation_rows(range(n_yz // 2, n_yz))
-    live[...] = jnp.transpose(jnp.broadcast_to(counts[...], (128, n_yz)))
-    for c in range(CHUNKS):
-        dense(c)
+    dense(CHUNKS - 1)
     to_scalar.wait()
     lane8 = lax.broadcasted_iota(jnp.int32, (8, 128), 1)
 

time: 49.9 us -> 49.5 us (level)
  no operation moved by 1% of the time
where the time goes in v4:
time: 49.5 us; the launch traced here: 49.4 us
  Pallas kernels  47.8 us (97%)
  local copies, waits for them, and re-layouts  1.62 us (3%)
    pallas_call x1, Pallas kernels, body(): pl.pallas_call(functools.partial(kernel, n_gx, n_yz), out_shape=jax.Shape...  47.8 us
    unnamed x1, local copies, waits for them, and re-layouts  1.62 us

profile of v4, /device:TPU:1, one launch (start us, length us, event | category | flops | bytes accessed | tf_op | source)
XLA Modules:
  0.0 49.4 jit_solution(9013449906122542340)
XLA Ops:
  0.0 47.8 %tidal.1 = f32[6,64,128]{2,1,0:T(8,128)} custom-call(f32[8,8,2048]{2,1,0:T(8,128)} %pot_hbm.1, s32[64,128]{1,0:T(8,128)} %bitcast.6, s32[64,128]{1,0:T(8,128)} %bitcast.7, s32[64,128]{1,0:T(8,128)} %bitcast.8, s32[1,64]{1,0:T(1,128)} %bitcast.9, bf16[384,2560]{1,0:T(8,128)(2,1)} %constant.4.clone.plane_hbm, bf16[3,1536,256]{2,1,0:T(8,128)(2,1)} %constant.5.clone.band_hbm), custom_call_target="tpu_custom_call" | custom-call | tf_op jit(solution)/shard_map/tidal/pallas_call | solution.py:344
  47.8 1.6 %copy.11 = f32[6,1,1,8192]{3,2,1,0:T(1,128)} copy(f32[6,1,1,8192]{3,2,1,0:T(1,128)} %bitcast.5) | data formatting | bytes 393216

commit v5 on v4

--- a/solution.py
+++ b/solution.py
@@ -175,7 +175,7 @@
             copy.start()
     for copy in x_copies[0]:
         copy.wait_send()
-    for copy in x_copies[1] + x_copies[2]:
+    for copy in x_copies[1] + x_copies[2] + x_copies[3]:
         copy.start()
     for to in in_plane:
         pl.semaphore_signal(ready, inc=1, device_id=to, device_id_type=MESH)
@@ -187,8 +187,6 @@
         remote(msg.at[to], slots.at[t], slot_send, slot_recv, (g, to)).start()
 
     pltpu.make_async_copy(msg.at[t], slots.at[t], slot_recv).start()
-    for copy in x_copies[3]:
-        copy.start()
 
     def corners(c):
         zs = pl.ds(c * zc, zc)

time: 49.5 us -> 49.5 us (level)
  no operation moved by 1% of the time
where the time goes in v5:
time: 49.5 us; the launch traced here: 49.4 us
  Pallas kernels  47.8 us (97%)
  local copies, waits for them, and re-layouts  1.62 us (3%)
    pallas_call x1, Pallas kernels, body(): pl.pallas_call(functools.partial(kernel, n_gx, n_yz), out_shape=jax.Shape...  47.8 us
    unnamed x1, local copies, waits for them, and re-layouts  1.62 us

profile of v5, /device:TPU:1, one launch (start us, length us, event | category | flops | bytes accessed | tf_op | source)
XLA Modules:
  0.0 49.4 jit_solution(12159198744781874757)
XLA Ops:
  0.0 47.8 %tidal.1 = f32[6,64,128]{2,1,0:T(8,128)} custom-call(f32[8,8,2048]{2,1,0:T(8,128)} %pot_hbm.1, s32[64,128]{1,0:T(8,128)} %bitcast.6, s32[64,128]{1,0:T(8,128)} %bitcast.7, s32[64,128]{1,0:T(8,128)} %bitcast.8, s32[1,64]{1,0:T(1,128)} %bitcast.9, bf16[384,2560]{1,0:T(8,128)(2,1)} %constant.4.clone.plane_hbm, bf16[3,1536,256]{2,1,0:T(8,128)(2,1)} %constant.5.clone.band_hbm), custom_call_target="tpu_custom_call" | custom-call | tf_op jit(solution)/shard_map/tidal/pallas_call | solution.py:342
  47.8 1.6 %copy.11 = f32[6,1,1,8192]{3,2,1,0:T(1,128)} copy(f32[6,1,1,8192]{3,2,1,0:T(1,128)} %bitcast.5) | data formatting | bytes 393216
